TPU v7x, 128 devices: a whole 4x4x4 slice. The times are simulated.
128 devices in a mesh: hst: 16 (over z, y_hi, core), local: 8 (over y_lo, x).
Axes of the slice: x: 4, y: 4 (y_hi: 2, y_lo: 2; y = y_hi * 2 + y_lo), z: 4, core: 2. Of those that a mesh axis runs over, the one named last changes fastest.
Arguments:
- pooled: bfloat16 [20480, 4096], P(('hst', 'local')), may hold values from -24 to 24
- cross_v: bfloat16 [512, 4096], replicated, may hold values from -0.09375 to 0.09375
- cross_u: bfloat16 [512, 4096], replicated, may hold values from -0.25 to 0.25
- cross_bias: float32 [4096], replicated, may hold values from -3 to 3
- head_weight: float32 [4096], replicated, may hold values from -0.09375 to 0.09375
- labels: int32 [20480], P(('hst', 'local')), may hold values from 0 to 1
- fn_weight: int32 [20480], P(('hst', 'local')), may hold values from 1 to 4
- row_ids: int32 [4, 32, 20480], P(None, 'hst'), may hold values from 0 to 8191
- bag_lengths: int32 [32, 20480], P('hst'), may hold values from 1 to 4
- table_rows: float32 [8192, 32, 128], P('local', 'hst'), may hold values from -6 to 6
- row_accum: float32 [8192, 32], P('local', 'hst'), may hold values from 0.0001 to 0.01
Outputs:
- grad_u: float32 [512, 4096], P(None, ('hst', 'local'))
- grad_v: float32 [512, 4096], P(None, ('hst', 'local'))
- grad_small: float32 [2, 4096], P(None, ('hst', 'local'))
- new_rows: float32 [8192, 32, 128], P('local', 'hst')
- new_accum: float32 [8192, 32], P('local', 'hst')
Inputs may be any that keep to these rules, and one draw needn't show every extreme that they name: `row_ids`: a row of the feature's table.
All inputs are finite; a program needn't handle non-finite values.
Results may differ from a plain program's by a relative error of at most 0.003.
The roundings to bfloat16 on the way count: a program that leaves them out, or rounds other values in their place, can miss the bound.
Values may be sent and summed in bfloat16 or wider, within the bound.
A program may use at most 128 MiB of HBM per device.

v0:
```python
import jax
import jax.numpy as jnp
from jax import lax
from jax.sharding import PartitionSpec as P

learn_rate = 0.05
epsilon = 1e-08


def contribute(grad_rows, ids_sel, lens_sel, begin_row, row_count):
    count_rows = grad_rows.shape[0]
    per_host = ids_sel.shape[1]
    width = grad_rows.shape[1] // per_host
    values = grad_rows.reshape(count_rows, per_host, width)
    row_iota = lax.broadcasted_iota(jnp.int32, (row_count, count_rows), 0)
    outputs = []
    for feature in range(per_host):
        counts = jnp.zeros((row_count, count_rows), jnp.bfloat16)
        for slot in range(ids_sel.shape[0]):
            local_row = ids_sel[slot, feature] - begin_row
            usable = slot < lens_sel[feature]
            target = jnp.where(usable, local_row, -1)
            counts = counts + (row_iota == target[None, :]).astype(jnp.bfloat16)
        outputs.append(jnp.dot(counts, values[:, feature, :], preferred_element_type=jnp.float32))
    return jnp.stack(outputs, axis=1)


def body(
    pooled,
    cross_v,
    cross_u,
    cross_bias,
    head_weight,
    labels,
    fn_weight,
    row_ids,
    bag_lengths,
    table_rows,
    row_accum,
):
    hidden = lax.dot_general(
        pooled, cross_v, (((1,), (1,)), ((), ())), preferred_element_type=jnp.float32
    ).astype(jnp.bfloat16)
    scale = jnp.dot(hidden, cross_u, preferred_element_type=jnp.float32) + cross_bias
    features = pooled.astype(jnp.float32)
    mixed = features * scale + features
    logits = jnp.sum(mixed * head_weight, axis=1)
    chance = jax.nn.sigmoid(logits)
    logit_grad = fn_weight.astype(jnp.float32) * (chance - labels.astype(jnp.float32))
    out_grad = logit_grad[:, None] * head_weight
    scale_grad = out_grad * features
    scale_half = scale_grad.astype(jnp.bfloat16)
    low_grad = lax.dot_general(
        scale_half, cross_u, (((1,), (1,)), ((), ())), preferred_element_type=jnp.float32
    ).astype(jnp.bfloat16)
    input_grad = (
        out_grad * (scale + 1.0) + jnp.dot(low_grad, cross_v, preferred_element_type=jnp.float32)
    ).astype(jnp.bfloat16)
    received = lax.all_to_all(input_grad, "hst", split_axis=1, concat_axis=0, tiled=True)
    part_u = lax.dot_general(
        hidden, scale_half, (((0,), (0,)), ((), ())), preferred_element_type=jnp.float32
    )
    part_v = lax.dot_general(
        low_grad, pooled, (((0,), (0,)), ((), ())), preferred_element_type=jnp.float32
    )
    part_small = jnp.stack(
        [jnp.sum(scale_grad, axis=0), jnp.sum(logit_grad[:, None] * mixed, axis=0)]
    )
    reduced = (
        lax.psum_scatter(part_u, ("hst", "local"), scatter_dimension=1, tiled=True),
        lax.psum_scatter(part_v, ("hst", "local"), scatter_dimension=1, tiled=True),
        lax.psum_scatter(part_small, ("hst", "local"), scatter_dimension=1, tiled=True),
    )
    host_count = lax.axis_size("hst")
    local_count = lax.axis_size("local")
    tok_rows = pooled.shape[0]
    slots = row_ids.shape[0]
    per_host = row_ids.shape[1]
    rows_dev = table_rows.shape[0]
    row_table = row_ids.reshape(slots, per_host, host_count, local_count, tok_rows)
    length_table = bag_lengths.reshape(per_host, host_count, local_count, tok_rows)
    ids_all = row_table.transpose(0, 1, 3, 2, 4).reshape(slots, per_host, -1)
    lens_all = length_table.transpose(0, 2, 1, 3).reshape(per_host, -1)
    my_start = lax.axis_index("local") * rows_dev
    row_grad = contribute(
        lax.all_gather(received, "local", axis=0, tiled=True), ids_all, lens_all, my_start, rows_dev
    )
    new_accum = row_accum + jnp.mean(row_grad * row_grad, axis=2)
    new_rows = table_rows - learn_rate * row_grad / (jnp.sqrt(new_accum)[:, :, None] + epsilon)
    return (reduced[0], reduced[1], reduced[2], new_rows, new_accum)


def solution(mesh):
    placed = (
        P(("hst", "local"), None),
        P(),
        P(),
        P(),
        P(),
        P(("hst", "local")),
        P(("hst", "local")),
        P(None, "hst", None),
        P("hst", None),
        P("local", "hst", None),
        P("local", "hst"),
    )
    return jax.shard_map(
        body,
        mesh=mesh,
        in_specs=placed,
        out_specs=(
            P(None, ("hst", "local")),
            P(None, ("hst", "local")),
            P(None, ("hst", "local")),
            P("local", "hst", None),
            P("local", "hst"),
        ),
        check_vma=False,
    )
```

profile of v0, /device:TPU:1, one launch (start us, length us, event | category | flops | bytes accessed | tf_op | source)
XLA Modules:
  0.0 2028.3 jit_solution(11719162177763341410)
XLA Ops:
  8.0 4.3 convolution_convert_fusion.1
  12.4 1.4 multiply_reduce_fusion.1
  13.8 1.6 convolution_convert_fusion
  15.4 1.5 copy-done.1
  16.9 1.0 fusion.32
  17.9 1.2 copy.48
  19.1 9.5 all-to-all-start
  28.6 2.5 fusion.33
  31.2 2.0 copy.32
  33.2 0.0 all-gather.2.cloned.1.call-start
  33.2 15.4 all-to-all-done
  48.6 1.1 copy-done.3
  49.8 4.7 fusion.42
  54.5 0.0 reduce-scatter.8.cloned.1.call-start
  54.5 4.7 fusion.46
  59.3 1.0 copy-done.6
  60.3 0.8 reshape.156
  61.1 0.3 copy.49
  61.5 0.9 reshape.157
  62.4 0.5 slice_subtract_fusion.7
  62.9 1.5 copy.30
  64.4 0.2 reshape.155
  64.6 0.1 copy.50
  64.7 0.2 slice_compare_fusion.7
  64.8 0.1 gt.95
  65.0 0.1 gt.93
  65.1 0.1 gt.91
  65.3 0.1 gt.89
  65.4 0.1 gt.87
  65.6 0.1 gt.85
  65.7 0.1 gt.83
  65.8 0.1 gt.81
  66.0 0.7 broadcast_select_fusion
  66.7 0.7 broadcast_select_fusion.2
  67.3 0.7 broadcast_select_fusion.4
  68.0 0.7 broadcast_select_fusion.6
  68.7 652.0 %reduce-scatter.10.cloned.1.call-done = f32[32,2]{1,0:T(8,128)} async-done(((f32[4096,2]{1,0:T(8,128)}), f32[32,2]{1,0:T(8,128)}) %reduce-scatter.10.cloned.1.call-update) | async-done | bytes 272
  720.7 1.4 copy.33
  722.1 15.3 reshape.158
  737.4 20.3 %fusion.45 = (bf16[20480,1,128]{2,1,0:T(2,128)(2,1)S(1)}, bf16[20480,1,128]{2,1,0:T(2,128)(2,1)S(1)}) fusion(bf16[20480,2,128]{2,1,0:T(2,128)(2,1)} %reshape.158), kind=kLoop, calls=%fused_computation.84 | loop fusion | bytes 20971520 | tf_op jit(solution)/shard_map/slice | solution.py:24
  757.7 46.5 %fusion.38 = f32[1024,1,128]{0,2,1:T(8,128)S(1)} fusion(bf16[20480,1,128]{2,1,0:T(2,128)(2,1)S(1)} %get-tuple-element.25, s32[20480]{0:T(1024)} %get-tuple-element.44, s32[20480]{0:T(1024)} %get-tuple-element.45, s32[20480]{0:T(1024)} %get-tuple-element.46, s32[20480]{0:T(1024)} %get-tuple-element.47), kind=kOutput, calls=%fused_computation.46 | convolution fusion | flops 5704253440 | bytes 6094848 | tf_op jit(solution)/shard_map/dot_general | solution.py:24
  804.2 44.9 %fusion.35 = f32[1024,1,128]{0,2,1:T(8,128)S(1)} fusion(bf16[20480,1,128]{2,1,0:T(2,128)(2,1)S(1)} %get-tuple-element.24, s32[20480]{0:T(1024)S(1)} %copy-done.9, s32[20480]{0:T(1024)S(1)} %copy-done.10, s32[20480]{0:T(1024)S(1)} %copy-done.11, s32[20480]{0:T(1024)S(1)} %copy-done.12), kind=kOutput, calls=%fused_computation.45 | convolution fusion | flops 5704253440 | bytes 6094848 | tf_op jit(solution)/shard_map/dot_general | solution.py:24
  849.2 0.1 multiply_reduce_fusion.2
  849.3 0.6 sqrt_add_fusion
  849.9 0.2 divide_subtract_fusion
  850.1 1.3 copy.31
  851.4 519.5 %reduce-scatter.6.cloned.1.call-done = f32[512,32]{0,1:T(8,128)} async-done(((f32[512,4096]{0,1:T(8,128)}), f32[512,32]{0,1:T(8,128)}) %reduce-scatter.6.cloned.1.call-update) | async-done | bytes 65552 | tf_op jit(solution)/shard_map/reduce_scatter | solution.py:70
  1370.9 650.2 %reduce-scatter.8.cloned.1.call-done = f32[512,32]{0,1:T(8,128)} async-done(((f32[512,4096]{0,1:T(8,128)}), f32[512,32]{0,1:T(8,128)}) %reduce-scatter.8.cloned.1.call-update) | async-done | bytes 65552 | tf_op jit(solution)/shard_map/reduce_scatter | solution.py:71
  (42 shorter events, 0.3 us)
Async XLA Ops:
  8.0 4.3 copy-start
  8.0 4.3 copy-start.8
  8.0 4.3 copy-start.17
  8.0 4.3 copy-start.16
  12.4 1.4 copy-start.14
  12.4 1.4 copy-start.15
  13.8 4.1 copy-start.2
  13.8 3.1 copy-start.1
  19.1 29.5 %all-to-all-start = ((bf16[160,16,256]{2,0,1:T(8,128)(2,1)}), bf16[160,16,256]{2,0,1:T(8,128)(2,1)S(1)}, u32[]{:S(2)}, u32[]{:S(2)}) async-start(bf16[160,16,256]{2,0,1:T(8,128)(2,1)} %bitcast.70), calls=%async_computation.2 | async-start | bytes 2621440 | tf_op jit(solution)/shard_map/all_to_all | solution.py:59
  28.6 692.1 %reduce-scatter.10.cloned.1.call-start = ((), (), s32[]{:S(2)}) async-start(), calls=%async_computation.7 | async-start | bytes 2113536
  33.2 688.9 %all-gather.2.cloned.1.call-start = ((), (), s32[]{:S(2)}) async-start(), calls=%async_computation.6 | async-start | bytes 11796480 | tf_op jit(solution)/shard_map/all_gather | solution.py:86
  48.6 1.1 copy-start.3
  49.7 1321.2 %reduce-scatter.6.cloned.1.call-start = ((), (), s32[]{:S(2)}) async-start(), calls=%async_computation.4 | async-start | bytes 8454144 | tf_op jit(solution)/shard_map/reduce_scatter | solution.py:70
  54.5 1966.6 %reduce-scatter.8.cloned.1.call-start = ((), (), s32[]{:S(2)}) async-start(), calls=%async_computation.5 | async-start | bytes 8454144 | tf_op jit(solution)/shard_map/reduce_scatter | solution.py:71
  59.3 1.1 copy-start.6
  59.3 3.6 copy-start.5
  60.3 4.0 copy-start.7
  757.6 46.5 %copy-start.9 = (s32[20480]{0:T(1024)S(1)}, s32[20480]{0:T(1024)}, u32[]{:S(2)}) copy-start(s32[20480]{0:T(1024)} %get-tuple-element.48) | copy-start | bytes 245764
  757.7 46.5 %copy-start.10 = (s32[20480]{0:T(1024)S(1)}, s32[20480]{0:T(1024)}, u32[]{:S(2)}) copy-start(s32[20480]{0:T(1024)} %get-tuple-element.49) | copy-start | bytes 245764
  757.7 46.5 %copy-start.11 = (s32[20480]{0:T(1024)S(1)}, s32[20480]{0:T(1024)}, u32[]{:S(2)}) copy-start(s32[20480]{0:T(1024)} %get-tuple-element.50) | copy-start | bytes 245764
  757.7 46.5 %copy-start.12 = (s32[20480]{0:T(1024)S(1)}, s32[20480]{0:T(1024)}, u32[]{:S(2)}) copy-start(s32[20480]{0:T(1024)} %get-tuple-element.51) | copy-start | bytes 245764
  804.2 45.1 %copy-start.13 = (f32[1024,2]{0,1:T(2,128)S(1)}, f32[1024,2]{0,1:T(2,128)}, u32[]{:S(2)}) copy-start(f32[1024,2]{0,1:T(2,128)} %param.21) | copy-start | bytes 24580
  804.2 45.7 %copy-start.4 = (f32[1024,2,128]{0,2,1:T(8,128)S(1)}, f32[1024,2,128]{0,2,1:T(8,128)}, u32[]{:S(2)}) copy-start(f32[1024,2,128]{0,2,1:T(8,128)} %copy.30) | copy-start | bytes 3145732
Sparse Core Ops, SparseCore 0:
  33.3 687.3 reduce-scatter.9
  723.8 647.1 reduce-scatter.5
  1373.9 647.2 reduce-scatter.7
Sparse Core Ops, SparseCore 1:
  49.8 109.8 all-gather.1
where the time goes:
time: 2040 us; the launch traced here: 2030 us
  waiting for transfers between devices  1840 us (90%)
  matrix products  109 us (5%)
  local copies, waits for them, and re-layouts  50.1 us (2%)
    unnamed x5, waiting for transfers between devices  652 us
    reduce_scatter x1, waiting for transfers between devices, body(): lax.psum_scatter(part_v, ('hst', 'local'), scatter_dimension=1, tiled=True)  650 us
    reduce_scatter x1, waiting for transfers between devices, body(): lax.psum_scatter(part_u, ('hst', 'local'), scatter_dimension=1, tiled=True)  520 us
    dot_general x2, matrix products, contribute(): jnp.dot(counts, values[:, feature, :], preferred_element_type=jnp.float32)  91.4 us
  transfers between devices with their start and end apart: 5, of which 4 were waited for; matrix products, arithmetic and copies ran while one was open for 8% of the time, Pallas kernels for 0%

commit v1 on v0

v1 whole, which is shorter than its diff:
```python
import jax
import jax.numpy as jnp
from jax import lax
from jax.experimental import pallas as pl
from jax.experimental.pallas import tpu as pltpu
from jax.sharding import PartitionSpec as P

learn_rate = 0.05
epsilon = 1e-08
MESH = pl.DeviceIdType.MESH
F32 = jnp.float32
BF16 = jnp.bfloat16

B = 160
R = 512
D = 4096
W = 256
G = 8
KC = G * B
RC = 1024
NT = (((1,), (1,)), ((), ()))
TN = (((0,), (0,)), ((), ()))

GROUP = [(2, 0), (2, 1), (1, 0), (3, 0), (1, 1), (3, 1), (0, 1), (0, 0)]
PLANE = [(kx, ka, kb) for kx in (2, 1, 3, 0) for ka in (1, 0) for kb in (1, 0)]


def kernel(
    pooled, v_hbm, u_hbm, bias, head, labels, fn_weight, ids,
    dense_out, small_out, rows_out,
    pool_v, v_v, u_v, scale_v, target, weight,
    pool_g, hid_g, low_g, lg_g, small_s, small_g,
    ig_s, e1, gath, half_g,
    dense_s, dense_r, tsmall_s, tsmall_r,
    acc, x_s, x_r,
    loc_sem, pg_s, pg_r, hg_s, hg_r, lo_s, lo_r, lg_s, lg_r, sm_s, sm_r,
    z_s, z_r, y_s, y_r, dn_s, dn_r, ts_s, ts_r, xs_s, xs_r,
):
    h = lax.axis_index("hst")
    l = lax.axis_index("local")
    z, yh, c = h // 4, (h // 2) % 2, h % 2
    yl, x = l // 4, l % 4
    me = z * 2 + c

    def group_dev(kz, kc):
        zz, cc = (z + kz) % 4, (c + kc) % 2
        return (zz * 4 + yh * 2 + cc, l), zz * 2 + cc

    def plane_dev(kx, ka, kb):
        hh, bb, xx = (yh + ka) % 2, (yl + kb) % 2, (x + kx) % 4
        return (z * 4 + hh * 2 + c, bb * 4 + xx), hh * W + (bb * 4 + xx) * 32

    def rcopy(src, dst, ss, rs, dev):
        return pltpu.make_async_remote_copy(
            src_ref=src, dst_ref=dst, send_sem=ss, recv_sem=rs, device_id=dev, device_id_type=MESH
        )

    barrier = pltpu.get_barrier_semaphore()
    for off in GROUP[:-1]:
        pl.semaphore_signal(barrier, inc=1, device_id=group_dev(*off)[0], device_id_type=MESH)
    for off in PLANE[:-1]:
        pl.semaphore_signal(barrier, inc=1, device_id=plane_dev(*off)[0], device_id_type=MESH)

    loads = [
        pltpu.make_async_copy(pooled, pool_v, loc_sem.at[0]),
        pltpu.make_async_copy(v_hbm, v_v, loc_sem.at[1]),
        pltpu.make_async_copy(u_hbm, u_v, loc_sem.at[2]),
    ]
    for ld in loads:
        ld.start()

    lane = lax.broadcasted_iota(jnp.int32, (8, 640), 1)
    for ys in range(4):
        for g in range(2):
            out = jnp.zeros((8, 640), jnp.int32)
            for i in range(4):
                hs = (2 * g + i // 2) * 4 + (ys // 2) * 2 + i % 2
                win = ids[:, pl.ds(hs * 1280 + (ys % 2) * 640, 640)]
                win = pltpu.roll(win, (160 * i + 640 - 160 * x) % 640, 1)
                out = jnp.where((lane >= 160 * i) & (lane < 160 * (i + 1)), win, out)
            target[:, pl.ds((ys * 2 + g) * 640, 640)] = out.astype(F32)
    for f in range(2):
        t = [target[pl.ds(f * 4 + s, 1), :] for s in range(4)]
        e01, e02, e03 = t[0] == t[1], t[0] == t[2], t[0] == t[3]
        e12, e13, e23 = t[1] == t[2], t[1] == t[3], t[2] == t[3]
        one = lambda m: jnp.where(m, 1.0, 0.0)
        weight[pl.ds(f * 4, 1), :] = 1.0 + one(e01) + one(e02) + one(e03)
        weight[pl.ds(f * 4 + 1, 1), :] = 1.0 + one(e12) + one(e13)
        weight[pl.ds(f * 4 + 2, 1), :] = 1.0 + one(e23)
        weight[pl.ds(f * 4 + 3, 1), :] = jnp.ones_like(t[0])
        target[pl.ds(f * 4 + 1, 1), :] = jnp.where(e01, -1.0, t[1])
        target[pl.ds(f * 4 + 2, 1), :] = jnp.where(e02 | e12, -1.0, t[2])
        target[pl.ds(f * 4 + 3, 1), :] = jnp.where(e03 | e13 | e23, -1.0, t[3])

    pl.semaphore_wait(barrier, len(GROUP) + len(PLANE) - 2)

    sends = []

    def go(copy):
        copy.start()
        sends.append(copy)
        return copy

    pg = []
    for k, off in enumerate(GROUP[:-1]):
        dev, m = group_dev(*off)
        for b in range(2):
            col = pl.multiple_of(((m // 2) * 4 + b * 2 + m % 2) * W, W)
            pg.append(go(rcopy(pooled.at[:, pl.ds(col, W)], pool_g.at[k, :, pl.ds(b * W, W)],
                               pg_s.at[k * 2 + b], pg_r.at[k * 2 + b], dev)))

    loads[0].wait()
    loads[1].wait()
    hid = lax.dot_general(pool_v[...], v_v[...], NT, preferred_element_type=F32).astype(BF16)
    hid_g[7] = hid
    hg = [go(rcopy(hid_g.at[7], hid_g.at[k], hg_s.at[k], hg_r.at[k], group_dev(*off)[0]))
          for k, off in enumerate(GROUP[:-1])]
    loads[2].wait()

    part = jnp.zeros((B, 128), F32)
    for j in range(8):
        cols = pl.ds(j * 512, 512)
        sc = jnp.dot(hid_g[7], u_v[:, cols], preferred_element_type=F32) + bias[:, cols]
        scale_v[:, cols] = sc
        f = pool_v[:, cols].astype(F32)
        prod = (f * sc + f) * head[:, cols]
        part = part + (prod[:, 0:128] + prod[:, 128:256]) + (prod[:, 256:384] + prod[:, 384:512])
    logits = jnp.sum(part, axis=1, keepdims=True)
    chance = 1.0 / (1.0 + jnp.exp(-logits))
    lg = fn_weight[...] * (chance - labels[...])
    lgb = jnp.broadcast_to(lg, (B, 128))
    lg_g[7] = lgb
    lgc = [go(rcopy(lg_g.at[7], lg_g.at[k], lg_s.at[k], lg_r.at[k], group_dev(*off)[0]))
           for k, off in enumerate(GROUP[:-1])]
    lgw = jnp.concatenate([lgb, lgb], axis=1)

    low = jnp.zeros((B, R), F32)
    for j in range(16):
        cols = pl.ds(j * W, W)
        f = pool_v[:, cols].astype(F32)
        sg = (lgw * head[:, cols]) * f
        low = low + lax.dot_general(sg.astype(BF16), u_v[:, cols], NT, preferred_element_type=F32)
        mixed = f * scale_v[:, cols] + f
        m, b = (j // 4) * 2 + j % 2, (j // 2) % 2
        small_s[m, b] = jnp.concatenate(
            [jnp.sum(sg, axis=0, keepdims=True), jnp.sum(lgw * mixed, axis=0, keepdims=True),
             jnp.zeros((6, W), F32)], axis=0)
    low_g[7] = low.astype(BF16)

    zc = []
    for k, off in enumerate(GROUP):
        dev, m = group_dev(*off)
        for b in range(2):
            cols = pl.ds(pl.multiple_of(((m // 2) * 4 + b * 2 + m % 2) * W, W), W)
            ig = (lgw * head[:, cols]) * (scale_v[:, cols] + 1.0) + jnp.dot(
                low_g[7], v_v[:, cols], preferred_element_type=F32)
            if k < 7:
                ig_s[k, b] = ig.astype(BF16)
            else:
                e1[me, b] = ig.astype(BF16)
        if k < 7:
            zc.append(go(rcopy(ig_s.at[k], e1.at[me], z_s.at[k], z_r.at[k], dev)))
    loc = [go(rcopy(low_g.at[7], low_g.at[k], lo_s.at[k], lo_r.at[k], group_dev(*off)[0]))
           for k, off in enumerate(GROUP[:-1])]
    smc = []
    for k, off in enumerate(GROUP[:-1]):
        dev, m = group_dev(*off)
        smc.append(go(rcopy(small_s.at[m], small_g.at[k], sm_s.at[k], sm_r.at[k], dev)))

    for cp in pg:
        cp.wait_recv()
    for b in range(2):
        col = pl.multiple_of(h // 4 * 4 * W + b * 2 * W + c * W, W)
        pool_g[7, :, pl.ds(b * W, W)] = pool_v[:, pl.ds(col, W)]
    for cp in lgc + hg:
        cp.wait_recv()
    for k in range(8):
        for b in range(2):
            col = pl.multiple_of(h // 4 * 4 * W + b * 2 * W + c * W, W)
            lgk = jnp.concatenate([lg_g[k], lg_g[k]], axis=1)
            half_g[pl.ds(k * B, B), pl.ds(b * W, W)] = (
                (lgk * head[:, pl.ds(col, W)]) * pool_g[k, :, pl.ds(b * W, W)].astype(F32)
            ).astype(BF16)
    dense_s[:, pl.ds(0, R)] = lax.dot_general(
        half_g[...], hid_g[...].reshape(KC, R), TN, preferred_element_type=F32).astype(BF16)

    yc = []

    def forward(src_m, j):
        gath[0, src_m] = e1[src_m, yh]
        for d in (1, 2, 3):
            ka, kb = d // 2, d % 2
            b = yh if ka == 0 else 1 - yh
            yc.append(go(rcopy(e1.at[src_m, b], gath.at[d, src_m], y_s.at[d - 1, j], y_r.at[d - 1, j],
                               plane_dev(0, ka, kb)[0])))

    forward(me, 7)
    for k in (6, 2, 3, 4, 5, 0, 1):
        zc[k].wait_recv()
        kz, kc = GROUP[k]
        forward(((z - kz + 4) % 4) * 2 + (c + kc) % 2, k)

    for cp in loc + smc:
        cp.wait_recv()
    dense_s[:, pl.ds(R, R)] = lax.dot_general(
        pool_g[...].reshape(KC, R), low_g[...].reshape(KC, R), TN, preferred_element_type=F32).astype(BF16)
    for b in range(2):
        tot = small_s[me, b]
        for k in range(7):
            tot = tot + small_g[k, b]
        tsmall_s[pl.ds(b * W, W), :] = jnp.concatenate([tot, jnp.zeros((120, W), F32)], axis=0).T
    dnc, tsc = [], []
    for k, off in enumerate(PLANE[:-1]):
        dev, row = plane_dev(*off)
        row = pl.multiple_of(row, 32)
        dnc.append(go(rcopy(dense_s.at[pl.ds(row, 32)], dense_r.at[k], dn_s.at[k], dn_r.at[k], dev)))
        tsc.append(go(rcopy(tsmall_s.at[pl.ds(row, 32)], tsmall_r.at[k], ts_s.at[k], ts_r.at[k], dev)))

    iota = lax.broadcasted_iota(jnp.int32, (16, KC), 0).astype(F32).astype(BF16)
    acc[...] = jnp.zeros_like(acc)

    def x_copy(kx):
        return rcopy(x_s.at[kx], x_r.at[kx], xs_s.at[kx], xs_r.at[kx], (h, yl * 4 + (x + kx + 1) % 4))

    def y_step(d, carry):
        @pl.when(d > 0)
        def _():
            def one_wait(j, cc):
                rcopy(e1.at[j, 0], gath.at[d, j], y_s.at[d - 1, j], y_r.at[d - 1, j], (h, l)).wait_recv()
                return cc
            lax.fori_loop(0, 8, one_wait, 0)

        src = ((yh + d // 2) % 2) * 2 + (yl + d % 2) % 2
        lanes = pl.ds(pl.multiple_of(src * KC, 128), KC)

        def chunk_step(kx, cc):
            base = (yl * 4 + (x + kx + 1) % 4) * RC
            for f in range(2):
                tt = [target[pl.ds(f * 4 + s, 1), lanes] for s in range(4)]
                ws = [jnp.broadcast_to(weight[pl.ds(f * 4 + s, 1), lanes], (16, KC)).astype(BF16)
                      for s in range(4)]
                tiles = []
                for sb in range(RC // 256):
                    low_row = (base + sb * 256).astype(F32)
                    ts = [jnp.broadcast_to(tt[s] - low_row, (16, KC)).astype(BF16) for s in range(4)]
                    for i in range(16):
                        it = iota + jnp.asarray(16 * i, BF16)
                        cnt = jnp.zeros((16, KC), BF16)
                        for s in range(4):
                            cnt = jnp.where(it == ts[s], ws[s], cnt)
                        tiles.append(cnt)
                counts = jnp.concatenate(tiles, axis=0)
                g = gath[d, :, :, pl.ds(f * 128, 128)].reshape(KC, 128)
                acc[kx, :, pl.ds(f * 128, 128)] += jnp.dot(counts, g, preferred_element_type=F32)

            @pl.when((d == 3) & (kx < 3))
            def _():
                x_s[kx] = acc[kx].astype(BF16)
                x_copy(kx).start()
            return cc

        return lax.fori_loop(0, 4, chunk_step, carry)

    lax.fori_loop(0, 4, y_step, 0)

    for cp in dnc + tsc:
        cp.wait_recv()
    dev, row = plane_dev(*PLANE[-1])
    row = pl.multiple_of(row, 32)
    tot = dense_s[pl.ds(row, 32)].astype(F32)
    small = tsmall_s[pl.ds(row, 32)]
    for k in range(15):
        tot = tot + dense_r[k].astype(F32)
        small = small + tsmall_r[k]
    dense_out[...] = tot
    small_out[...] = small

    for kx in range(3):
        x_copy(kx).wait_recv()
    rows_out[...] = acc[3] + (x_r[0].astype(F32) + x_r[1].astype(F32)) + x_r[2].astype(F32)
    for kx in range(3):
        x_copy(kx).wait_send()
    for cp in sends:
        cp.wait_send()


def fused(pooled, cross_v, cross_u, bias, head, labels, fn_weight, ids):
    any_, vmem = pl.BlockSpec(memory_space=pl.ANY), pl.BlockSpec(memory_space=pltpu.VMEM)
    V, S = pltpu.VMEM, lambda *n: pltpu.SemaphoreType.DMA(n)
    return pl.pallas_call(
        kernel,
        out_shape=(
            jax.ShapeDtypeStruct((32, 2 * R), F32),
            jax.ShapeDtypeStruct((32, 128), F32),
            jax.ShapeDtypeStruct((RC, W), F32),
        ),
        in_specs=[any_, any_, any_, vmem, vmem, vmem, vmem, vmem],
        out_specs=(vmem, vmem, vmem),
        scratch_shapes=[
            V((B, D), BF16), V((R, D), BF16), V((R, D), BF16), V((B, D), F32),
            V((8, 4 * KC), F32), V((8, 4 * KC), F32),
            V((G, B, R), BF16), V((G, B, R), BF16), V((G, B, R), BF16), V((G, B, 128), F32),
            V((G, 2, 8, W), F32), V((G, 2, 8, W), F32),
            V((G - 1, 2, B, W), BF16), V((G, 2, B, W), BF16), V((4, G, B, W), BF16), V((KC, R), BF16),
            V((R, 2 * R), BF16), V((15, 32, 2 * R), BF16), V((R, 128), F32), V((15, 32, 128), F32),
            V((4, RC, W), F32), V((3, RC, W), BF16), V((3, RC, W), BF16),
            S(3), S(14), S(14), S(7), S(7), S(7), S(7), S(7), S(7), S(7), S(7),
            S(7), S(7), S(3, 8), S(3, 8), S(15), S(15), S(15), S(15), S(3), S(3),
        ],
        compiler_params=pltpu.CompilerParams(
            collective_id=0, has_side_effects=True, vmem_limit_bytes=58 * 2**20
        ),
        cost_estimate=pl.CostEstimate(flops=16 * 10**9, bytes_accessed=12 * 10**6, transcendentals=160),
    )(pooled, cross_v, cross_u, bias, head, labels, fn_weight, ids)


def body(
    pooled, cross_v, cross_u, cross_bias, head_weight, labels, fn_weight,
    row_ids, bag_lengths, table_rows, row_accum,
):
    slot = lax.broadcasted_iota(jnp.int32, row_ids.shape, 0)
    live = jnp.where(slot < bag_lengths[None], row_ids, -1)
    ids = live.transpose(1, 0, 2).reshape(8, -1)
    dense, small, row_grad = fused(
        pooled, cross_v, cross_u, cross_bias[None], head_weight[None],
        labels.astype(F32)[:, None], fn_weight.astype(F32)[:, None], ids,
    )
    row_grad = row_grad.reshape(RC, 2, 128)
    new_accum = row_accum + jnp.mean(row_grad * row_grad, axis=2)
    new_rows = table_rows - learn_rate * row_grad / (jnp.sqrt(new_accum)[:, :, None] + epsilon)
    return (dense[:, :R].T, dense[:, R:].T, small[:, :2].T, new_rows, new_accum)


def solution(mesh):
    placed = (
        P(("hst", "local"), None), P(), P(), P(), P(), P(("hst", "local")), P(("hst", "local")),
        P(None, "hst", None), P("hst", None), P("local", "hst", None), P("local", "hst"),
    )
    both = P(None, ("hst", "local"))
    return jax.shard_map(
        body, mesh=mesh, in_specs=placed,
        out_specs=(both, both, both, P("local", "hst", None), P("local", "hst")),
        check_vma=False,
    )
```

time: 2040 us -> 149 us (0.07)
  waiting for transfers between devices: 1840 us -> 0 us
  Pallas kernels: 0 us -> 131 us
  matrix products: 109 us -> 0 us
  local copies, waits for them, and re-layouts: 50.1 us -> 6.4 us
    reduce_scatter x2 -> x0, waiting for transfers between devices: 1170 us -> none  [the longest x1 650 us: body(): lax.psum_scatter(part_v, ('hst', 'local'), scatter_dimension=1, tiled=True)]
    unnamed x5 -> x0, waiting for transfers between devices: 652 us -> none
    pallas_call x0 -> x1, Pallas kernels: none -> 131 us  [fused(): pl.pallas_call(kernel, out_shape=(jax.ShapeDtypeStruct((32, 2 * R), F32),...]
    dot_general x8 -> x0, matrix products: 109 us -> none  [the longest x2 91.4 us: contribute(): jnp.dot(counts, values[:, feature, :], preferred_element_type=jnp.float32)]
  transfers between devices with their start and end apart: 5 -> 0, of which waited for: 4 -> 0; matrix products, arithmetic and copies ran while one was open for 8% -> 0% of each run, Pallas kernels for 0% -> 0%
where the time goes in v1:
time: 149 us
  Pallas kernels  131 us (88%)
  other arithmetic  10 us (7%)
  local copies, waits for them, and re-layouts  6.4 us (4%)
    pallas_call x1, Pallas kernels, fused(): pl.pallas_call(kernel, out_shape=(jax.ShapeDtypeStruct((32, 2 * R), F32),...  131 us
    sub x1, other arithmetic, body(): table_rows - learn_rate * row_grad / (jnp.sqrt(new_accum)[:, :, None] + e...  4.44 us

profile of v1, /device:TPU:1, one launch (start us, length us, event | category | flops | bytes accessed | tf_op | source)
XLA Modules:
  0.0 148.7 jit_solution(9813147965552986937)
XLA Ops:
  0.6 1.5 %fusion = s32[2,4,20480]{2,0,1:T(2,128)S(1)} fusion(s32[4,2,20480]{2,1,0:T(2,128)} %param.18, s32[2,20480]{1,0:T(2,128)} %param.19), kind=kLoop, calls=%fused_computation.2 | loop fusion | flops 327680 | bytes 1474560 | tf_op jit(solution)/shard_map/transpose | solution.py:323
  2.2 0.4 copy.24
  2.6 1.1 reshape.20.ids
  3.7 0.7 convert_element_type.6
  4.3 0.8 copy.25.labels
  5.1 0.7 convert_element_type.7
  5.8 0.8 copy.26.fn_weight
  6.5 131.5 %shard_map.146 = (f32[32,1024]{1,0:T(8,128)}, f32[32,128]{1,0:T(8,128)}, f32[1024,256]{1,0:T(8,128)}) custom-call(bf16[160,4096]{1,0:T(8,128)(2,1)} %pooled.1, bf16[512,4096]{1,0:T(8,128)(2,1)} %v_hbm.1, bf16[512,4096]{1,0:T(8,128)(2,1)} %u_hbm.1, f32[1,4096]{1,0:T(1,128)} %bitcast.14, f32[1,4096]{1,0:T(1,128)} %bitcast.15, f32[160,1]{1,0:T(8,128)} %copy.25.labels, ...), custom_call_target="tpu_custom_call" | custom-call | flops 16000000000 | bytes 12000000 | tf_op jit(solution)/shard_map/pallas_call | solution.py:290
  138.0 0.0 copy-start.2
  138.0 1.4 broadcast_multiply_fusion
  139.4 0.5 mul.19
  140.0 1.1 reduce_sum.9
  141.1 0.0 copy-done.2
  141.1 0.2 copy.27
  141.4 0.0 copy-start
  141.4 0.0 copy-start.1
  141.4 0.2 sqrt_add_fusion
  141.6 0.5 mul.17
  142.1 4.4 %divide_subtract_fusion = f32[1024,2,128]{2,1,0:T(2,128)} fusion(f32[1024,2,128]{2,1,0:T(2,128)} %param.20, f32[1024,2,128]{2,1,0:T(2,128)S(1)} %mul.17, f32[1024,2]{1,0:T(8,128)S(1)} %get-tuple-element.26), kind=kLoop, calls=%fused_computation.1 | loop fusion | flops 524288 | bytes 3153920 | tf_op jit(solution)/shard_map/sub | solution.py:330
  146.6 0.8 copy.29
  147.4 0.0 copy-done
  147.4 0.7 slice_bitcast_fusion
  148.0 0.0 copy-done.1
  148.0 0.6 copy.28
  (1 shorter events, 0.0 us)
Async XLA Ops:
  138.0 3.1 %copy-start.2 = (f32[1024,2]{0,1:T(2,128)S(1)}, f32[1024,2]{0,1:T(2,128)}, u32[]{:S(2)}) copy-start(f32[1024,2]{0,1:T(2,128)} %param.21) | copy-start | bytes 24580
  141.4 6.0 %copy-start = (f32[32,1024]{1,0:T(8,128)S(1)}, f32[32,1024]{1,0:T(8,128)}, u32[]{:S(2)}) copy-start(f32[32,1024]{1,0:T(8,128)} %get-tuple-element.8) | copy-start | bytes 393220
  141.4 6.6 %copy-start.1 = (f32[32,128]{1,0:T(8,128)S(1)}, f32[32,128]{1,0:T(8,128)}, u32[]{:S(2)}) copy-start(f32[32,128]{1,0:T(8,128)} %get-tuple-element.9) | copy-start | bytes 49156

commit v2 on v0

v2 whole, which is shorter than its diff:
```python
import jax
import jax.numpy as jnp
from jax import lax
from jax.experimental import pallas as pl
from jax.experimental.pallas import tpu as pltpu
from jax.sharding import PartitionSpec as P

learn_rate = 0.05
epsilon = 1e-08
MESH = pl.DeviceIdType.MESH
F32 = jnp.float32
BF16 = jnp.bfloat16

B = 160
R = 512
D = 4096
W = 256
E = 128
G = 8
KC = G * B
RC = 1024
NT = (((1,), (1,)), ((), ()))
TN = (((0,), (0,)), ((), ()))

GROUP = [(2, 0), (2, 1), (1, 0), (3, 0), (1, 1), (3, 1), (0, 1)]
ARRIVE = [(0, 1), (1, 0), (3, 0), (1, 1), (3, 1), (2, 0), (2, 1)]
YS = [(0, 1), (1, 0), (1, 1)]
DENSE = [(2, 0), (2, 1), (1, 0), (3, 0), (1, 1), (3, 1), (0, 1)]


def kernel(
    pooled, v_hbm, u_hbm, bias, head, labels, fn_weight, ids_hbm, lens_hbm, table_hbm, accum,
    out_u, out_v, out_small, out_rows, out_accum,
    pool_v, v_v, u_v, scale_v, ids, lens, table, target, weight, cols_v,
    pool_g, hid_g, low_g, lg_g, small_s, small_g,
    ig_s, e1, gath, half_g,
    dense_s, dense_r, tsmall_s, tsmall_r, d2_s, d2_r, d3_r,
    acc, x_s, x_r,
    loc_sem, pg_s, pg_r, hg_s, hg_r, lo_s, lo_r, lg_s, lg_r, sm_s, sm_r,
    z_s, z_r, y1_s, y1_r, y3_s, y3_r, y2_s, y2_r, dn_s, dn_r, ts_s, ts_r, d2_ss, d2_rs, d3_ss, d3_rs, xs_s, xs_r,
):
    h = lax.axis_index("hst")
    l = lax.axis_index("local")
    z, yh, c = h // 4, (h // 2) % 2, h % 2
    yl, x = l // 4, l % 4
    me = z * 2 + c

    def group_dev(kz, kc):
        zz, cc = (z + kz) % 4, (c + kc) % 2
        return (zz * 4 + yh * 2 + cc, l), zz * 2 + cc

    def y_dev(ka, kb):
        return (z * 4 + ((yh + ka) % 2) * 2 + c, ((yl + kb) % 2) * 4 + x)

    def x_dev(kx):
        return (h, yl * 4 + (x + kx) % 4)

    def dense_dev(kx, kc):
        xx, cc = (x + kx) % 4, (c + kc) % 2
        return (z * 4 + yh * 2 + cc, yl * 4 + xx), xx * 2 + cc

    def dense_cols(m, zt):
        col = (zt * 4 + (m // 4) * 2 + m % 2) * W + ((m // 2) % 2) * E
        return pl.ds(pl.multiple_of(col, E), E)

    def rcopy(src, dst, ss, rs, dev):
        return pltpu.make_async_remote_copy(
            src_ref=src, dst_ref=dst, send_sem=ss, recv_sem=rs, device_id=dev, device_id_type=MESH
        )

    def src_of(kz, kc):
        return ((z - kz + 4) % 4) * 2 + (c + kc) % 2

    barrier = pltpu.get_barrier_semaphore()
    partners = [group_dev(*o)[0] for o in GROUP] + [y_dev(*o) for o in YS] + [dense_dev(*o)[0] for o in DENSE[:-1]]
    for dev in partners:
        pl.semaphore_signal(barrier, inc=1, device_id=dev, device_id_type=MESH)

    def load(src, dst, i):
        cp = pltpu.make_async_copy(src, dst, loc_sem.at[i])
        cp.start()
        return cp

    ld_ids, ld_lens = load(ids_hbm, ids, 0), load(lens_hbm, lens, 1)
    ld_pool, ld_v, ld_u = load(pooled, pool_v, 2), load(v_hbm, v_v, 3), load(u_hbm, u_v, 4)
    ld_table = load(table_hbm, table, 5)

    cols_v[...] = jnp.zeros_like(cols_v)
    cols_v[pl.ds(0, 1), pl.ds(0, B)] = labels[...].astype(F32)
    cols_v[pl.ds(1, 1), pl.ds(0, B)] = fn_weight[...].astype(F32)

    def column(row):
        return jnp.broadcast_to(row, (128, row.shape[1])).T

    lab_c = column(cols_v[pl.ds(0, 1), :])[:B]
    fnw_c = column(cols_v[pl.ds(1, 1), :])[:B]

    pl.semaphore_wait(barrier, len(partners))

    sends = []

    def go(copy):
        copy.start()
        sends.append(copy)
        return copy

    pg = []
    for k, (kx, kc) in enumerate(DENSE):
        dev, m = dense_dev(kx, kc)
        for zt in range(4):
            pg.append(go(rcopy(pooled.at[:, dense_cols(m, zt)], pool_g.at[kc * 4 + kx, :, pl.ds(zt * E, E)],
                               pg_s.at[k * 4 + zt], pg_r.at[k * 4 + zt], dev)))

    def spread(buf, ss, rs):
        def far(kx):
            return rcopy(buf.at[0], buf.at[kx], ss.at[kx], rs.at[kx], dense_dev(kx, 0)[0])

        def near(kx):
            return rcopy(buf.at[kx], buf.at[4 + kx], ss.at[4 + kx], rs.at[4 + kx], dense_dev(0, 1)[0])

        for kx in (2, 1, 3):
            far(kx).start()
        near(0).start()

        def relay():
            for kx in (1, 3, 2):
                far(kx).wait_recv()
                near(kx).start()

        def finish():
            for kx in range(4):
                near(kx).wait_recv()

        def drain():
            for kx in range(4):
                near(kx).wait_send()
            for kx in (1, 2, 3):
                far(kx).wait_send()

        return relay, finish, drain

    ld_pool.wait()
    ld_v.wait()
    hid_g[0] = lax.dot_general(pool_v[...], v_v[...], NT, preferred_element_type=F32).astype(BF16)
    hid_relay, hid_finish, hid_drain = spread(hid_g, hg_s, hg_r)
    ld_u.wait()

    part = jnp.zeros((B, 128), F32)
    for j in range(8):
        cols = pl.ds(j * 512, 512)
        sc = jnp.dot(hid_g[0], u_v[:, cols], preferred_element_type=F32) + bias[:, cols]
        scale_v[:, cols] = sc
        f = pool_v[:, cols].astype(F32)
        prod = (f * sc + f) * head[:, cols]
        part = part + (prod[:, 0:128] + prod[:, 128:256]) + (prod[:, 256:384] + prod[:, 384:512])
    logits = jnp.sum(part, axis=1, keepdims=True)
    chance = 1.0 / (1.0 + jnp.exp(-jnp.broadcast_to(logits, (B, 128))))
    lgb = fnw_c * (chance - lab_c)
    lg_row = jnp.concatenate([lgb, jnp.zeros((96, 128), F32)], axis=0).T[:8]
    lg_g[0] = lg_row
    lgc = [go(rcopy(lg_g.at[0], lg_g.at[kc * 4 + kx], lg_s.at[k], lg_r.at[k], dense_dev(kx, kc)[0]))
           for k, (kx, kc) in enumerate(DENSE)]
    lgw = jnp.concatenate([lgb, lgb], axis=1)

    low = jnp.zeros((B, R), F32)
    for j in range(16):
        cols = pl.ds(j * W, W)
        f = pool_v[:, cols].astype(F32)
        sg = (lgw * head[:, cols]) * f
        low = low + lax.dot_general(sg.astype(BF16), u_v[:, cols], NT, preferred_element_type=F32)
        mixed = f * scale_v[:, cols] + f
        sums = jnp.concatenate(
            [jnp.sum(sg, axis=0, keepdims=True), jnp.sum(lgw * mixed, axis=0, keepdims=True),
             jnp.zeros((6, W), F32)], axis=0)
        for b in range(2):
            m = (((j // 2) % 2) * 2 + b) * 2 + j % 2
            small_s[m, :, pl.ds((j // 4) * E, E)] = sums[:, b * E:(b + 1) * E]
    low_g[0] = low.astype(BF16)
    low_relay, low_finish, low_drain = spread(low_g, lo_s, lo_r)

    def z_copy(f, k, dev):
        return rcopy(ig_s.at[f, k], e1.at[f, me], z_s.at[f, k], z_r.at[f, k], dev)

    for k, off in enumerate(GROUP + [(0, 0)]):
        dev, m = group_dev(*off)
        for b in range(2):
            cols = pl.ds(pl.multiple_of(((m // 2) * 4 + b * 2 + m % 2) * W, W), W)
            ig = ((lgw * head[:, cols]) * (scale_v[:, cols] + 1.0) + jnp.dot(
                low_g[0], v_v[:, cols], preferred_element_type=F32)).astype(BF16)
            for f in range(2):
                if k < 7:
                    ig_s[f, k, b] = ig[:, f * E:(f + 1) * E]
                else:
                    e1[f, me, b] = ig[:, f * E:(f + 1) * E]
        if k < 7:
            go(z_copy(0, k, dev))
    for k, off in enumerate(GROUP):
        go(z_copy(1, k, group_dev(*off)[0]))
    smc = []
    for k, (kx, kc) in enumerate(DENSE):
        dev, m = dense_dev(kx, kc)
        smc.append(go(rcopy(small_s.at[m], small_g.at[k], sm_s.at[k], sm_r.at[k], dev)))

    def y1_copy(f, m):
        return rcopy(e1.at[f, m, yh], gath.at[f, 1, m], y1_s.at[f, m], y1_r.at[f, m], y_dev(0, 1))

    def y3_copy(f, m):
        return rcopy(e1.at[f, m, 1 - yh], gath.at[f, 3, m], y3_s.at[f, m], y3_r.at[f, m], y_dev(1, 1))

    def y2_copy(f, m):
        return rcopy(gath.at[f, 3, m], gath.at[f, 2, m], y2_s.at[f, m], y2_r.at[f, m], y_dev(0, 1))

    def forward(f, m):
        y3_copy(f, m).start()
        y1_copy(f, m).start()
        gath[f, 0, m] = e1[f, m, yh]

    def forward_all(f, order):
        for kz, kc in order:
            z_copy(f, GROUP.index((kz, kc)), (h, l)).wait_recv()
            forward(f, src_of(kz, kc))

    def relay_all(f):
        for kz, kc in [(0, 0)] + ARRIVE:
            m = src_of(kz, kc)
            y3_copy(f, m).wait_recv()
            y2_copy(f, m).start()

    forward(0, me)
    forward_all(0, ARRIVE[:1])
    forward(1, me)

    ld_ids.wait()
    ld_lens.wait()
    lane = lax.broadcasted_iota(jnp.int32, (8, 640), 1)
    for ys in range(4):
        for g in range(2):
            out = jnp.zeros((8, 640), jnp.int32)
            for i in range(4):
                hs = (2 * g + i // 2) * 4 + (ys // 2) * 2 + i % 2
                win = pl.ds(hs * 1280 + (ys % 2) * 640, 640)
                ln = lens[:, win]
                got = jnp.concatenate([jnp.where(ln > s, ids[s, :, win], -1) for s in range(4)], axis=0)
                got = pltpu.roll(got, (160 * i + 640 - 160 * x) % 640, 1)
                out = jnp.where((lane >= 160 * i) & (lane < 160 * (i + 1)), got, out)
            target[:, pl.ds((ys * 2 + g) * 640, 640)] = out.astype(F32)
    for f in range(2):
        t = [target[pl.ds(s * 2 + f, 1), :] for s in range(4)]
        e01, e02, e03 = t[0] == t[1], t[0] == t[2], t[0] == t[3]
        e12, e13, e23 = t[1] == t[2], t[1] == t[3], t[2] == t[3]
        one = lambda m: jnp.where(m, 1.0, 0.0)
        weight[pl.ds(f, 1), :] = 1.0 + one(e01) + one(e02) + one(e03)
        weight[pl.ds(2 + f, 1), :] = 1.0 + one(e12) + one(e13)
        weight[pl.ds(4 + f, 1), :] = 1.0 + one(e23)
        weight[pl.ds(6 + f, 1), :] = jnp.ones_like(t[0])
        target[pl.ds(2 + f, 1), :] = jnp.where(e01, -1.0, t[1])
        target[pl.ds(4 + f, 1), :] = jnp.where(e02 | e12, -1.0, t[2])
        target[pl.ds(6 + f, 1), :] = jnp.where(e03 | e13 | e23, -1.0, t[3])

    forward_all(0, ARRIVE[1:])
    acc[...] = jnp.zeros_like(acc)

    def d1_copies(k):
        kz = (2, 1, 3)[k]
        dev, zz = group_dev(kz, 0)[0], (z + kz) % 4
        return (rcopy(dense_s.at[zz], dense_r.at[k], dn_s.at[k], dn_r.at[k], dev),
                rcopy(tsmall_s.at[zz], tsmall_r.at[k], ts_s.at[k], ts_r.at[k], dev))

    def dense_products():
        mine = x * 2 + c
        own_cols = [dense_cols(mine, zt) for zt in range(4)]
        for zt in range(4):
            pool_g[0, :, pl.ds(zt * E, E)] = pool_v[:, own_cols[zt]]
        own_head = jnp.concatenate([head[:, own_cols[zt]] for zt in range(4)], axis=1)

        for cp in pg + lgc:
            cp.wait_recv()
        hid_finish()
        for k in range(8):
            lgk = jnp.concatenate([lg_g[k]] * 16, axis=0).T[:B]
            lgk = jnp.concatenate([lgk] * 4, axis=1)
            half_g[pl.ds(k * B, B), :] = ((lgk * own_head) * pool_g[k].astype(F32)).astype(BF16)
        dense_s[:, :, :, pl.ds(0, R)] = lax.dot_general(
            half_g[...], hid_g[...].reshape(KC, R), TN, preferred_element_type=F32
        ).astype(BF16).reshape(4, 4, 32, R)
        low_finish()
        ld_table.wait()
        for cp in smc:
            cp.wait_recv()
        dense_s[:, :, :, pl.ds(R, R)] = lax.dot_general(
            pool_g[...].reshape(KC, R), low_g[...].reshape(KC, R), TN, preferred_element_type=F32
        ).astype(BF16).reshape(4, 4, 32, R)
        tot = small_s[mine]
        for k in range(7):
            tot = tot + small_g[k]
        tsmall_s[...] = jnp.concatenate([tot, jnp.zeros((120, R), F32)], axis=0).T.reshape(4, 4, 32, 128)
        for k in range(3):
            for cp in d1_copies(k):
                cp.start()

    iota = lax.broadcasted_iota(jnp.int32, (16, KC), 0).astype(F32).astype(BF16)

    def x_off(kx):
        return (2 - kx + (kx // 2) * 3 + (kx // 3) * 2) % 4

    def x_copy(f, kx):
        return rcopy(x_s.at[f, kx], x_r.at[f, kx], xs_s.at[f, kx], xs_r.at[f, kx], x_dev(x_off(kx)))

    def d2_copy(k):
        xx = (x + k + 1) % 4
        return rcopy(d2_s.at[xx], d2_r.at[x], d2_ss.at[k], d2_rs.at[k], x_dev(k + 1))

    def d3_copy(k):
        ka, kb = YS[k]
        yy = ((yh + ka) % 2) * 2 + (yl + kb) % 2
        return rcopy(d2_r.at[yy], d3_r.at[k], d3_ss.at[k], d3_rs.at[k], y_dev(ka, kb))

    def update(f):
        for kx in range(3):
            x_copy(f, kx).wait_recv()
        g = acc[3, :, pl.ds(f * E, E)] + (x_r[f, 0].astype(F32) + x_r[f, 1].astype(F32)) + x_r[f, 2].astype(F32)
        new = column(accum[pl.ds(f, 1), :]) + jnp.sum(g * g, axis=1, keepdims=True) * (1.0 / E)
        rows = pl.ds(f, RC, stride=2)
        out_rows[rows, :] = table[rows, :] - learn_rate * g / (jnp.sqrt(new) + epsilon)
        out_accum[pl.ds(f, 1), :] = new.T[:1]

    def step(s, carry):
        f, dd = s // 4, s % 4
        d = dd + (dd // 2) * (1 - 2 * (dd % 2))

        @pl.when(s == 1)
        def _():
            relay_all(0)
            forward_all(1, ARRIVE)

        @pl.when(s == 2)
        def _():
            hid_relay()

        @pl.when(s == 3)
        def _():
            low_relay()
            relay_all(1)

        @pl.when(s == 4)
        def _():
            dense_products()

        @pl.when(s == 6)
        def _():
            for k in range(3):
                for cp in d1_copies(k):
                    cp.wait_recv()
            d2_s[:, :, pl.ds(0, 2 * R)] = (
                (dense_s[z].astype(F32) + dense_r[0].astype(F32))
                + (dense_r[1].astype(F32) + dense_r[2].astype(F32)))
            d2_s[:, :, pl.ds(2 * R, 128)] = (tsmall_s[z] + tsmall_r[0]) + (tsmall_r[1] + tsmall_r[2])
            d2_r[x] = d2_s[x]
            for k in range(3):
                d2_copy(k).start()

        @pl.when(s == 7)
        def _():
            for k in range(3):
                d2_copy(k).wait_recv()
            for k in range(3):
                d3_copy(k).start()
            update(0)

        @pl.when(dd == 1)
        def _():
            def one(m, cc):
                y1_copy(f, m).wait_recv()
                return cc
            lax.fori_loop(0, 8, one, 0)

        @pl.when(dd == 3)
        def _():
            def one(m, cc):
                y2_copy(f, m).wait_recv()
                return cc
            lax.fori_loop(0, 8, one, 0)

        src = ((yh + d // 2) % 2) * 2 + (yl + d % 2) % 2
        lanes = pl.ds(pl.multiple_of(src * KC, 128), KC)
        fcols = pl.ds(pl.multiple_of(f * E, E), E)

        def chunk_step(kx, cc):
            base = (yl * 4 + (x + x_off(kx)) % 4) * RC
            tt = [target[pl.ds(q * 2 + f, 1), lanes] for q in range(4)]
            ws = [jnp.broadcast_to(weight[pl.ds(q * 2 + f, 1), lanes], (16, KC)).astype(BF16)
                  for q in range(4)]
            tiles = []
            for sb in range(RC // 256):
                low_row = (base + sb * 256).astype(F32)
                ts = [jnp.broadcast_to(tt[q] - low_row, (16, KC)).astype(BF16) for q in range(4)]
                for i in range(16):
                    it = iota + jnp.asarray(16 * i, BF16)
                    cnt = jnp.zeros((16, KC), BF16)
                    for q in range(4):
                        cnt = jnp.where(it == ts[q], ws[q], cnt)
                    tiles.append(cnt)
            counts = jnp.concatenate(tiles, axis=0)
            g = gath[f, d].reshape(KC, E)
            acc[kx, :, fcols] += jnp.dot(counts, g, preferred_element_type=F32)

            @pl.when((dd == 3) & (kx < 3))
            def _():
                x_s[f, kx] = acc[kx, :, fcols].astype(BF16)
                x_copy(f, kx).start()
            return cc

        return lax.fori_loop(0, 4, chunk_step, carry)

    lax.fori_loop(0, 8, step, 0)

    for k in range(3):
        d3_copy(k).wait_recv()
    tot = (d2_r[yh * 2 + yl] + d3_r[0]) + (d3_r[1] + d3_r[2])
    out_u[...] = tot[:, :R]
    out_v[...] = tot[:, R:2 * R]
    out_small[...] = tot[:, 2 * R:]
    update(1)

    for f in range(2):
        for kx in range(3):
            x_copy(f, kx).wait_send()

        def drain(m, cc):
            y1_copy(f, m).wait_send()
            y3_copy(f, m).wait_send()
            y2_copy(f, m).wait_send()
            return cc
        lax.fori_loop(0, 8, drain, 0)
    for k in range(3):
        d2_copy(k).wait_send()
        d3_copy(k).wait_send()
        for cp in d1_copies(k):
            cp.wait_send()
    hid_drain()
    low_drain()
    for cp in sends:
        cp.wait_send()


def fused(*operands):
    any_, vmem = pl.BlockSpec(memory_space=pl.ANY), pl.BlockSpec(memory_space=pltpu.VMEM)
    V, S = pltpu.VMEM, lambda *n: pltpu.SemaphoreType.DMA(n)
    return pl.pallas_call(
        kernel,
        out_shape=(
            jax.ShapeDtypeStruct((32, R), F32),
            jax.ShapeDtypeStruct((32, R), F32),
            jax.ShapeDtypeStruct((32, 128), F32),
            jax.ShapeDtypeStruct((2 * RC, E), F32),
            jax.ShapeDtypeStruct((2, RC), F32),
        ),
        in_specs=[any_, any_, any_, vmem, vmem, vmem, vmem, any_, any_, any_, vmem],
        out_specs=(vmem,) * 5,
        scratch_shapes=[
            V((B, D), BF16), V((R, D), BF16), V((R, D), BF16), V((B, D), F32),
            V((4, 2, 20480), jnp.int32), V((2, 20480), jnp.int32), V((2 * RC, E), F32),
            V((8, 4 * KC), F32), V((8, 4 * KC), F32), V((8, 256), F32),
            V((G, B, R), BF16), V((G, B, R), BF16), V((G, B, R), BF16), V((G, 8, 256), F32),
            V((G, 8, R), F32), V((G - 1, 8, R), F32),
            V((2, G - 1, 2, B, E), BF16), V((2, G, 2, B, E), BF16), V((2, 4, G, B, E), BF16), V((KC, R), BF16),
            V((4, 4, 32, 2 * R), BF16), V((3, 4, 32, 2 * R), BF16),
            V((4, 4, 32, 128), F32), V((3, 4, 32, 128), F32),
            V((4, 32, 2 * R + 128), F32), V((4, 32, 2 * R + 128), F32), V((3, 32, 2 * R + 128), F32),
            V((4, RC, W), F32), V((2, 3, RC, E), BF16), V((2, 3, RC, E), BF16),
            S(6), S(28), S(28), S(8), S(8), S(8), S(8), S(7), S(7), S(7), S(7),
            S(2, 7), S(2, 7), S(2, 8), S(2, 8), S(2, 8), S(2, 8), S(2, 8), S(2, 8),
            S(3), S(3), S(3), S(3), S(3), S(3), S(3), S(3), S(2, 3), S(2, 3),
        ],
        compiler_params=pltpu.CompilerParams(
            collective_id=0, has_side_effects=True, vmem_limit_bytes=60 * 2**20
        ),
        cost_estimate=pl.CostEstimate(flops=16 * 10**9, bytes_accessed=12 * 10**6, transcendentals=160),
    )(*operands)


def body(
    pooled, cross_v, cross_u, cross_bias, head_weight, labels, fn_weight,
    row_ids, bag_lengths, table_rows, row_accum,
):
    grad_u, grad_v, small, rows, accum = fused(
        pooled, cross_v, cross_u, cross_bias[None], head_weight[None], labels[None], fn_weight[None],
        row_ids, bag_lengths, table_rows.reshape(2 * RC, E), row_accum.T,
    )
    return grad_u.T, grad_v.T, small[:, :2].T, rows.reshape(RC, 2, E), accum.T


def solution(mesh):
    placed = (
        P(("hst", "local"), None), P(), P(), P(), P(), P(("hst", "local")), P(("hst", "local")),
        P(None, "hst", None), P("hst", None), P("local", "hst", None), P("local", "hst"),
    )
    both = P(None, ("hst", "local"))
    return jax.shard_map(
        body, mesh=mesh, in_specs=placed,
        out_specs=(both, both, both, P("local", "hst", None), P("local", "hst")),
        check_vma=False,
    )
```

time: 2040 us -> 100 us (0.05)
  waiting for transfers between devices: 1840 us -> 0 us
  matrix products: 109 us -> 0 us
  Pallas kernels: 0 us -> 91.1 us
  local copies, waits for them, and re-layouts: 50.1 us -> 7.86 us
    reduce_scatter x2 -> x0, waiting for transfers between devices: 1170 us -> none  [the longest x1 650 us: body(): lax.psum_scatter(part_v, ('hst', 'local'), scatter_dimension=1, tiled=True)]
    unnamed x5 -> x0, waiting for transfers between devices: 652 us -> none
    dot_general x8 -> x0, matrix products: 109 us -> none  [the longest x2 91.4 us: contribute(): jnp.dot(counts, values[:, feature, :], preferred_element_type=jnp.float32)]
    pallas_call x0 -> x1, Pallas kernels: none -> 91.1 us  [fused(): pl.pallas_call(kernel, out_shape=(jax.ShapeDtypeStruct((32, R), F32), jax...]
  transfers between devices with their start and end apart: 5 -> 0, of which waited for: 4 -> 0; matrix products, arithmetic and copies ran while one was open for 8% -> 0% of each run, Pallas kernels for 0% -> 0%
where the time goes in v2:
time: 100 us; the launch traced here: 99.6 us
  Pallas kernels  91.1 us (91%)
  local copies, waits for them, and re-layouts  7.86 us (8%)
    pallas_call x1, Pallas kernels, fused(): pl.pallas_call(kernel, out_shape=(jax.ShapeDtypeStruct((32, R), F32), jax...  91.1 us
    unnamed x5, local copies, waits for them, and re-layouts  7.14 us

profile of v2, /device:TPU:1, one launch (start us, length us, event | category | flops | bytes accessed | tf_op | source)
XLA Modules:
  0.0 99.6 jit_solution(3637051945835292284)
XLA Ops:
  0.6 91.1 %shard_map.146 = (f32[32,512]{1,0:T(8,128)}, f32[32,512]{1,0:T(8,128)}, f32[32,128]{1,0:T(8,128)}, f32[2048,128]{1,0:T(8,128)}, f32[2,1024]{1,0:T(2,128)}) custom-call(bf16[160,4096]{1,0:T(8,128)(2,1)} %pooled.1, bf16[512,4096]{1,0:T(8,128)(2,1)} %v_hbm.1, bf16[512,4096]{1,0:T(8,128)(2,1)} %u_hbm.1, f32[1,4096]{1,0:T(1,128)} %bitcast.17, ...), custom_call_target="tpu_custom_call" | custom-call | flops 16000000000 | bytes 12000000 | tf_op jit(solution)/shard_map/pallas_call | solution.py:449
  91.8 0.7 slice_bitcast_fusion
  92.5 0.6 copy.16
  93.1 1.5 %copy.21 = f32[512,32]{0,1:T(8,128)} copy(f32[512,32]{0,1:T(8,128)} %bitcast.14) | data formatting | bytes 131072
  94.6 1.5 %copy.22 = f32[512,32]{0,1:T(8,128)} copy(f32[512,32]{0,1:T(8,128)} %bitcast.13) | data formatting | bytes 131072
  96.1 2.3 %copy.23 = f32[1024,2,128]{2,1,0:T(2,128)} copy(f32[1024,2,128]{2,1,0:T(2,128)} %bitcast.12) | data formatting | bytes 2097152
  98.3 1.3 %copy.24 = f32[1024,2]{0,1:T(2,128)} copy(f32[1024,2]{0,1:T(2,128)} %bitcast.15) | data formatting | bytes 16384

commit v3 on v2

--- a/solution.py
+++ b/solution.py
@@ -24,14 +24,15 @@
 
 GROUP = [(2, 0), (2, 1), (1, 0), (3, 0), (1, 1), (3, 1), (0, 1)]
 ARRIVE = [(0, 1), (1, 0), (3, 0), (1, 1), (3, 1), (2, 0), (2, 1)]
+NEAR = [(0, 0)]
 YS = [(0, 1), (1, 0), (1, 1)]
 DENSE = [(2, 0), (2, 1), (1, 0), (3, 0), (1, 1), (3, 1), (0, 1)]
 
 
 def kernel(
-    pooled, v_hbm, u_hbm, bias, head, labels, fn_weight, ids_hbm, lens_hbm, table_hbm, accum,
-    out_u, out_v, out_small, out_rows, out_accum,
-    pool_v, v_v, u_v, scale_v, ids, lens, table, target, weight, cols_v,
+    pooled, v_hbm, u_hbm, bias, head, labels, fn_weight, ids_hbm, lens_hbm,
+    out_dense, out_rows,
+    pool_v, v_v, u_v, scale_v, ids, lens, target, weight, cols_v,
     pool_g, hid_g, low_g, lg_g, small_s, small_g,
     ig_s, e1, gath, half_g,
     dense_s, dense_r, tsmall_s, tsmall_r, d2_s, d2_r, d3_r,
@@ -81,9 +82,7 @@
         cp.start()
         return cp
 
-    ld_ids, ld_lens = load(ids_hbm, ids, 0), load(lens_hbm, lens, 1)
     ld_pool, ld_v, ld_u = load(pooled, pool_v, 2), load(v_hbm, v_v, 3), load(u_hbm, u_v, 4)
-    ld_table = load(table_hbm, table, 5)
 
     cols_v[...] = jnp.zeros_like(cols_v)
     cols_v[pl.ds(0, 1), pl.ds(0, B)] = labels[...].astype(F32)
@@ -138,6 +137,8 @@
                 far(kx).wait_send()
 
         return relay, finish, drain
+
+    ld_ids, ld_lens = load(ids_hbm, ids, 0), load(lens_hbm, lens, 1)
 
     ld_pool.wait()
     ld_v.wait()
@@ -194,8 +195,6 @@
                     e1[f, me, b] = ig[:, f * E:(f + 1) * E]
         if k < 7:
             go(z_copy(0, k, dev))
-    for k, off in enumerate(GROUP):
-        go(z_copy(1, k, group_dev(*off)[0]))
     smc = []
     for k, (kx, kc) in enumerate(DENSE):
         dev, m = dense_dev(kx, kc)
@@ -220,8 +219,8 @@
             z_copy(f, GROUP.index((kz, kc)), (h, l)).wait_recv()
             forward(f, src_of(kz, kc))
 
-    def relay_all(f):
-        for kz, kc in [(0, 0)] + ARRIVE:
+    def relay_all(f, order):
+        for kz, kc in order:
             m = src_of(kz, kc)
             y3_copy(f, m).wait_recv()
             y2_copy(f, m).start()
@@ -258,6 +257,8 @@
         target[pl.ds(6 + f, 1), :] = jnp.where(e03 | e13 | e23, -1.0, t[3])
 
     forward_all(0, ARRIVE[1:])
+    for k, off in enumerate(GROUP):
+        go(z_copy(1, k, group_dev(*off)[0]))
     acc[...] = jnp.zeros_like(acc)
 
     def d1_copies(k):
@@ -284,7 +285,6 @@
             half_g[...], hid_g[...].reshape(KC, R), TN, preferred_element_type=F32
         ).astype(BF16).reshape(4, 4, 32, R)
         low_finish()
-        ld_table.wait()
         for cp in smc:
             cp.wait_recv()
         dense_s[:, :, :, pl.ds(R, R)] = lax.dot_general(
@@ -293,7 +293,8 @@
         tot = small_s[mine]
         for k in range(7):
             tot = tot + small_g[k]
-        tsmall_s[...] = jnp.concatenate([tot, jnp.zeros((120, R), F32)], axis=0).T.reshape(4, 4, 32, 128)
+        for zt in range(4):
+            tsmall_s[zt] = tot[:, zt * E:(zt + 1) * E]
         for k in range(3):
             for cp in d1_copies(k):
                 cp.start()
@@ -315,112 +316,96 @@
         yy = ((yh + ka) % 2) * 2 + (yl + kb) % 2
         return rcopy(d2_r.at[yy], d3_r.at[k], d3_ss.at[k], d3_rs.at[k], y_dev(ka, kb))
 
-    def update(f):
+    def row_sums(f):
         for kx in range(3):
             x_copy(f, kx).wait_recv()
-        g = acc[3, :, pl.ds(f * E, E)] + (x_r[f, 0].astype(F32) + x_r[f, 1].astype(F32)) + x_r[f, 2].astype(F32)
-        new = column(accum[pl.ds(f, 1), :]) + jnp.sum(g * g, axis=1, keepdims=True) * (1.0 / E)
-        rows = pl.ds(f, RC, stride=2)
-        out_rows[rows, :] = table[rows, :] - learn_rate * g / (jnp.sqrt(new) + epsilon)
-        out_accum[pl.ds(f, 1), :] = new.T[:1]
-
-    def step(s, carry):
+        out_rows[:, pl.ds(f * E, E)] = (
+            acc[3, :, pl.ds(f * E, E)] + (x_r[f, 0].astype(F32) + x_r[f, 1].astype(F32)) + x_r[f, 2].astype(F32))
+
+    def wait_y(copy, f):
+        def one(m, cc):
+            copy(f, m).wait_recv()
+            return cc
+        lax.fori_loop(0, 8, one, 0)
+
+    def sum_along_z():
+        for k in range(3):
+            for cp in d1_copies(k):
+                cp.wait_recv()
+        d2_s[:, :, pl.ds(0, 2 * R)] = (
+            (dense_s[z].astype(F32) + dense_r[0].astype(F32))
+            + (dense_r[1].astype(F32) + dense_r[2].astype(F32)))
+        few = (tsmall_s[z] + tsmall_r[0]) + (tsmall_r[1] + tsmall_r[2])
+        d2_s[:, :, pl.ds(2 * R, 128)] = jnp.concatenate(
+            [few, jnp.zeros((120, 128), F32)], axis=0).T.reshape(4, 32, 128)
+        d2_r[x] = d2_s[x]
+        for k in range(3):
+            d2_copy(k).start()
+
+    def blocks_along_y():
+        for k in range(3):
+            d2_copy(k).wait_recv()
+        for k in range(3):
+            d3_copy(k).start()
+
+    def at(t, when, act):
+        pl.when(t == when)(act)
+
+    def step(t, carry):
+        late = t // 24
+        s = (1 - late) * (t // 4) + late * (6 + t % 2)
+        kx = (1 - late) * (t % 4) + late * ((t - 24) // 2)
         f, dd = s // 4, s % 4
         d = dd + (dd // 2) * (1 - 2 * (dd % 2))
-
-        @pl.when(s == 1)
-        def _():
-            relay_all(0)
-            forward_all(1, ARRIVE)
-
-        @pl.when(s == 2)
-        def _():
-            hid_relay()
-
-        @pl.when(s == 3)
-        def _():
-            low_relay()
-            relay_all(1)
-
-        @pl.when(s == 4)
-        def _():
-            dense_products()
-
-        @pl.when(s == 6)
-        def _():
-            for k in range(3):
-                for cp in d1_copies(k):
-                    cp.wait_recv()
-            d2_s[:, :, pl.ds(0, 2 * R)] = (
-                (dense_s[z].astype(F32) + dense_r[0].astype(F32))
-                + (dense_r[1].astype(F32) + dense_r[2].astype(F32)))
-            d2_s[:, :, pl.ds(2 * R, 128)] = (tsmall_s[z] + tsmall_r[0]) + (tsmall_r[1] + tsmall_r[2])
-            d2_r[x] = d2_s[x]
-            for k in range(3):
-                d2_copy(k).start()
-
-        @pl.when(s == 7)
-        def _():
-            for k in range(3):
-                d2_copy(k).wait_recv()
-            for k in range(3):
-                d3_copy(k).start()
-            update(0)
-
-        @pl.when(dd == 1)
-        def _():
-            def one(m, cc):
-                y1_copy(f, m).wait_recv()
-                return cc
-            lax.fori_loop(0, 8, one, 0)
-
-        @pl.when(dd == 3)
-        def _():
-            def one(m, cc):
-                y2_copy(f, m).wait_recv()
-                return cc
-            lax.fori_loop(0, 8, one, 0)
+        at(t, 1, lambda: relay_all(0, NEAR + ARRIVE))
+        at(t, 4, lambda: wait_y(y1_copy, 0))
+        at(t, 7, lambda: forward_all(1, ARRIVE))
+        at(t, 10, hid_relay)
+        at(t, 11, lambda: relay_all(1, NEAR + ARRIVE[:3]))
+        at(t, 12, lambda: wait_y(y2_copy, 0))
+        at(t, 12, low_relay)
+        at(t, 13, dense_products)
+        at(t, 15, lambda: relay_all(1, ARRIVE[3:]))
+        at(t, 20, lambda: wait_y(y1_copy, 1))
+        at(t, 24, sum_along_z)
+        at(t, 24, lambda: wait_y(y2_copy, 1))
+        at(t, 30, blocks_along_y)
+        at(t, 30, lambda: row_sums(0))
 
         src = ((yh + d // 2) % 2) * 2 + (yl + d % 2) % 2
         lanes = pl.ds(pl.multiple_of(src * KC, 128), KC)
         fcols = pl.ds(pl.multiple_of(f * E, E), E)
 
-        def chunk_step(kx, cc):
-            base = (yl * 4 + (x + x_off(kx)) % 4) * RC
-            tt = [target[pl.ds(q * 2 + f, 1), lanes] for q in range(4)]
-            ws = [jnp.broadcast_to(weight[pl.ds(q * 2 + f, 1), lanes], (16, KC)).astype(BF16)
-                  for q in range(4)]
-            tiles = []
-            for sb in range(RC // 256):
-                low_row = (base + sb * 256).astype(F32)
-                ts = [jnp.broadcast_to(tt[q] - low_row, (16, KC)).astype(BF16) for q in range(4)]
-                for i in range(16):
-                    it = iota + jnp.asarray(16 * i, BF16)
-                    cnt = jnp.zeros((16, KC), BF16)
-                    for q in range(4):
-                        cnt = jnp.where(it == ts[q], ws[q], cnt)
-                    tiles.append(cnt)
-            counts = jnp.concatenate(tiles, axis=0)
-            g = gath[f, d].reshape(KC, E)
-            acc[kx, :, fcols] += jnp.dot(counts, g, preferred_element_type=F32)
-
-            @pl.when((dd == 3) & (kx < 3))
-            def _():
-                x_s[f, kx] = acc[kx, :, fcols].astype(BF16)
-                x_copy(f, kx).start()
-            return cc
-
-        return lax.fori_loop(0, 4, chunk_step, carry)
-
-    lax.fori_loop(0, 8, step, 0)
+        base = (yl * 4 + (x + x_off(kx)) % 4) * RC
+        tt = [target[pl.ds(q * 2 + f, 1), lanes] for q in range(4)]
+        ws = [jnp.broadcast_to(weight[pl.ds(q * 2 + f, 1), lanes], (16, KC)).astype(BF16)
+              for q in range(4)]
+        tiles = []
+        for sb in range(RC // 256):
+            low_row = (base + sb * 256).astype(F32)
+            ts = [jnp.broadcast_to(tt[q] - low_row, (16, KC)).astype(BF16) for q in range(4)]
+            for i in range(16):
+                it = iota + jnp.asarray(16 * i, BF16)
+                cnt = jnp.zeros((16, KC), BF16)
+                for q in range(4):
+                    cnt = jnp.where(it == ts[q], ws[q], cnt)
+                tiles.append(cnt)
+        counts = jnp.concatenate(tiles, axis=0)
+        g = gath[f, d].reshape(KC, E)
+        acc[kx, :, fcols] += jnp.dot(counts, g, preferred_element_type=F32)
+
+        @pl.when((dd == 3) & (kx < 3))
+        def _():
+            x_s[f, kx] = acc[kx, :, fcols].astype(BF16)
+            x_copy(f, kx).start()
+        return carry
+
+    lax.fori_loop(0, 32, step, 0)
 
     for k in range(3):
         d3_copy(k).wait_recv()
-    tot = (d2_r[yh * 2 + yl] + d3_r[0]) + (d3_r[1] + d3_r[2])
-    out_u[...] = tot[:, :R]
-    out_v[...] = tot[:, R:2 * R]
-    out_small[...] = tot[:, 2 * R:]
-    update(1)
+    out_dense[...] = (d2_r[yh * 2 + yl] + d3_r[0]) + (d3_r[1] + d3_r[2])
+    row_sums(1)
 
     for f in range(2):
         for kx in range(3):
@@ -448,27 +433,21 @@
     V, S = pltpu.VMEM, lambda *n: pltpu.SemaphoreType.DMA(n)
     return pl.pallas_call(
         kernel,
-        out_shape=(
-            jax.ShapeDtypeStruct((32, R), F32),
-            jax.ShapeDtypeStruct((32, R), F32),
-            jax.ShapeDtypeStruct((32, 128), F32),
-            jax.ShapeDtypeStruct((2 * RC, E), F32),
-            jax.ShapeDtypeStruct((2, RC), F32),
-        ),
-        in_specs=[any_, any_, any_, vmem, vmem, vmem, vmem, any_, any_, any_, vmem],
-        out_specs=(vmem,) * 5,
+        out_shape=(jax.ShapeDtypeStruct((32, 2 * R + 128), F32), jax.ShapeDtypeStruct((RC, W), F32)),
+        in_specs=[any_, any_, any_, vmem, vmem, vmem, vmem, any_, any_],
+        out_specs=(vmem, vmem),
         scratch_shapes=[
             V((B, D), BF16), V((R, D), BF16), V((R, D), BF16), V((B, D), F32),
-            V((4, 2, 20480), jnp.int32), V((2, 20480), jnp.int32), V((2 * RC, E), F32),
+            V((4, 2, 20480), jnp.int32), V((2, 20480), jnp.int32),
             V((8, 4 * KC), F32), V((8, 4 * KC), F32), V((8, 256), F32),
             V((G, B, R), BF16), V((G, B, R), BF16), V((G, B, R), BF16), V((G, 8, 256), F32),
             V((G, 8, R), F32), V((G - 1, 8, R), F32),
             V((2, G - 1, 2, B, E), BF16), V((2, G, 2, B, E), BF16), V((2, 4, G, B, E), BF16), V((KC, R), BF16),
             V((4, 4, 32, 2 * R), BF16), V((3, 4, 32, 2 * R), BF16),
-            V((4, 4, 32, 128), F32), V((3, 4, 32, 128), F32),
+            V((4, 8, 128), F32), V((3, 8, 128), F32),
             V((4, 32, 2 * R + 128), F32), V((4, 32, 2 * R + 128), F32), V((3, 32, 2 * R + 128), F32),
             V((4, RC, W), F32), V((2, 3, RC, E), BF16), V((2, 3, RC, E), BF16),
-            S(6), S(28), S(28), S(8), S(8), S(8), S(8), S(7), S(7), S(7), S(7),
+            S(5), S(28), S(28), S(8), S(8), S(8), S(8), S(7), S(7), S(7), S(7),
             S(2, 7), S(2, 7), S(2, 8), S(2, 8), S(2, 8), S(2, 8), S(2, 8), S(2, 8),
             S(3), S(3), S(3), S(3), S(3), S(3), S(3), S(3), S(2, 3), S(2, 3),
         ],
@@ -479,15 +458,60 @@
     )(*operands)
 
 
+def finish_kernel(dense, rg, table, accum, out_u, out_v, out_small, out_rows, out_accum):
+    @pl.when(pl.program_id(0) == 0)
+    def _():
+        out_u[...] = dense[:, pl.ds(0, R)]
+        out_v[...] = dense[:, pl.ds(R, R)]
+        few = jnp.concatenate([dense[:, pl.ds(2 * R, 128)], jnp.zeros((96, 128), F32)], axis=0).T
+        out_small[...] = few[:2, :32]
+
+    n = rg.shape[0]
+    for f in range(2):
+        g = rg[:, pl.ds(f * E, E)]
+        old = jnp.broadcast_to(accum[pl.ds(f, 1), :], (128, n)).T
+        new = old + jnp.sum(g * g, axis=1, keepdims=True) * (1.0 / E)
+        rows = pl.ds(f, n, stride=2)
+        out_rows[rows, :] = table[rows, :] - learn_rate * g / (jnp.sqrt(new) + epsilon)
+        out_accum[pl.ds(f, 1), :] = new.T[:1]
+
+
+def finish(dense, rg, table, accum):
+    steps = 4
+    n = RC // steps
+    whole = lambda *shape: pl.BlockSpec(shape, lambda i: (0, 0))
+    return pl.pallas_call(
+        finish_kernel,
+        grid=(steps,),
+        out_shape=(
+            jax.ShapeDtypeStruct((32, R), F32),
+            jax.ShapeDtypeStruct((32, R), F32),
+            jax.ShapeDtypeStruct((2, 32), F32),
+            jax.ShapeDtypeStruct((2 * RC, E), F32),
+            jax.ShapeDtypeStruct((2, RC), F32),
+        ),
+        in_specs=[
+            whole(32, 2 * R + 128), pl.BlockSpec((n, W), lambda i: (i, 0)),
+            pl.BlockSpec((2 * n, E), lambda i: (i, 0)), pl.BlockSpec((2, n), lambda i: (0, i)),
+        ],
+        out_specs=(
+            whole(32, R), whole(32, R), whole(2, 32),
+            pl.BlockSpec((2 * n, E), lambda i: (i, 0)), pl.BlockSpec((2, n), lambda i: (0, i)),
+        ),
+        cost_estimate=pl.CostEstimate(flops=4 * 10**6, bytes_accessed=3 * 2**20, transcendentals=2**18),
+    )(dense, rg, table, accum)
+
+
 def body(
     pooled, cross_v, cross_u, cross_bias, head_weight, labels, fn_weight,
     row_ids, bag_lengths, table_rows, row_accum,
 ):
-    grad_u, grad_v, small, rows, accum = fused(
+    dense, row_grad = fused(
         pooled, cross_v, cross_u, cross_bias[None], head_weight[None], labels[None], fn_weight[None],
-        row_ids, bag_lengths, table_rows.reshape(2 * RC, E), row_accum.T,
+        row_ids, bag_lengths,
     )
-    return grad_u.T, grad_v.T, small[:, :2].T, rows.reshape(RC, 2, E), accum.T
+    grad_u, grad_v, small, rows, accum = finish(dense, row_grad, table_rows.reshape(2 * RC, E), row_accum.T)
+    return grad_u.T, grad_v.T, small, rows.reshape(RC, 2, E), accum.T
 
 
 def solution(mesh):

time: 100 us -> 88.5 us (0.89)
  local copies, waits for them, and re-layouts: 7.86 us -> 0 us
  Pallas kernels: 91.1 us -> 87.6 us
    unnamed x5 -> x0, local copies, waits for them, and re-layouts: 7.14 us -> none
    pallas_call x1 -> x2, Pallas kernels: 91.1 us -> 87.6 us  [the longest x1 83.1 us: fused(): pl.pallas_call(kernel, out_shape=(jax.ShapeDtypeStruct((32, 2 * R + 128),...]
where the time goes in v3:
time: 88.5 us; the launch traced here: 88.3 us
  Pallas kernels  87.6 us (99%)
    pallas_call x1, Pallas kernels, fused(): pl.pallas_call(kernel, out_shape=(jax.ShapeDtypeStruct((32, 2 * R + 128),...  83.1 us
    pallas_call x1, Pallas kernels, finish(): pl.pallas_call(finish_kernel, grid=(steps,), out_shape=(jax.ShapeDtypeStr...  4.49 us

profile of v3, /device:TPU:1, one launch (start us, length us, event | category | flops | bytes accessed | tf_op | source)
XLA Modules:
  0.0 88.3 jit_solution(178975164665844351)
XLA Ops:
  0.6 83.1 %shard_map.146 = (f32[32,1152]{1,0:T(8,128)}, f32[1024,256]{1,0:T(8,128)}) custom-call(bf16[160,4096]{1,0:T(8,128)(2,1)} %pooled.1, bf16[512,4096]{1,0:T(8,128)(2,1)} %v_hbm.1, bf16[512,4096]{1,0:T(8,128)(2,1)} %u_hbm.1, f32[1,4096]{1,0:T(1,128)} %bitcast.15, f32[1,4096]{1,0:T(1,128)} %bitcast.16, s32[1,160]{1,0:T(1,128)} %bitcast.18, s32[1,160]{1,0:T(1,128)} %bitcast.19, ...), custom_call_target="tpu_custom_call" | custom-call | flops 16000000000 | bytes 12000000 | tf_op jit(solution)/shard_map/pallas_call | solution.py:434
  83.8 4.5 %shard_map.147 = (f32[32,512]{1,0:T(8,128)}, f32[32,512]{1,0:T(8,128)}, f32[2,32]{1,0:T(2,128)}, f32[2048,128]{1,0:T(8,128)}, f32[2,1024]{1,0:T(2,128)}) custom-call(f32[32,1152]{1,0:T(8,128)} %get-tuple-element.12.dense, f32[1024,256]{1,0:T(8,128)} %get-tuple-element.13.rg, f32[2048,128]{1,0:T(8,128)} %bitcast.10, f32[2,1024]{1,0:T(2,128)} %bitcast.11), custom_call_target="tpu_custom_call" | custom-call | flops 4000000 | bytes 3145728 | tf_op jit(solution)/shard_map/pallas_call | solution.py:483

commit v4 on v3

--- a/solution.py
+++ b/solution.py
@@ -477,7 +477,7 @@
 
 
 def finish(dense, rg, table, accum):
-    steps = 4
+    steps = 2
     n = RC // steps
     whole = lambda *shape: pl.BlockSpec(shape, lambda i: (0, 0))
     return pl.pallas_call(

time: 88.5 us -> 87.4 us (0.988)
  Pallas kernels: 87.6 us -> 86.6 us
    pallas_call x1, Pallas kernels: 4.49 us -> 3.42 us  [finish(): pl.pallas_call(finish_kernel, grid=(steps,), out_shape=(jax.ShapeDtypeStr...]
where the time goes in v4:
time: 87.4 us; the launch traced here: 87.2 us
  Pallas kernels  86.6 us (99%)
    pallas_call x1, Pallas kernels, fused(): pl.pallas_call(kernel, out_shape=(jax.ShapeDtypeStruct((32, 2 * R + 128),...  83.1 us
    pallas_call x1, Pallas kernels, finish(): pl.pallas_call(finish_kernel, grid=(steps,), out_shape=(jax.ShapeDtypeStr...  3.42 us

profile of v4, /device:TPU:1, one launch (start us, length us, event | category | flops | bytes accessed | tf_op | source)
XLA Modules:
  0.0 87.2 jit_solution(13214278973268862091)
XLA Ops:
  0.6 83.1 %shard_map.146 = (f32[32,1152]{1,0:T(8,128)}, f32[1024,256]{1,0:T(8,128)}) custom-call(bf16[160,4096]{1,0:T(8,128)(2,1)} %pooled.1, bf16[512,4096]{1,0:T(8,128)(2,1)} %v_hbm.1, bf16[512,4096]{1,0:T(8,128)(2,1)} %u_hbm.1, f32[1,4096]{1,0:T(1,128)} %bitcast.15, f32[1,4096]{1,0:T(1,128)} %bitcast.16, s32[1,160]{1,0:T(1,128)} %bitcast.18, s32[1,160]{1,0:T(1,128)} %bitcast.19, ...), custom_call_target="tpu_custom_call" | custom-call | flops 16000000000 | bytes 12000000 | tf_op jit(solution)/shard_map/pallas_call | solution.py:434
  83.8 3.4 %shard_map.147 = (f32[32,512]{1,0:T(8,128)}, f32[32,512]{1,0:T(8,128)}, f32[2,32]{1,0:T(2,128)}, f32[2048,128]{1,0:T(8,128)}, f32[2,1024]{1,0:T(2,128)}) custom-call(f32[32,1152]{1,0:T(8,128)} %get-tuple-element.12.dense, f32[1024,256]{1,0:T(8,128)} %get-tuple-element.13.rg, f32[2048,128]{1,0:T(8,128)} %bitcast.10, f32[2,1024]{1,0:T(2,128)} %bitcast.11), custom_call_target="tpu_custom_call" | custom-call | flops 4000000 | bytes 3145728 | tf_op jit(solution)/shard_map/pallas_call | solution.py:483
